TPU v7x, 32 devices: a whole 2x2x4 slice. The times are simulated.
32 devices in a mesh: dp: 8 (over z, y), tensor: 4 (over x, core).
Axes of the slice: x: 2, y: 2, z: 4, core: 2. Of those that a mesh axis runs over, the one named last changes fastest.
Arguments:
- tokens: bfloat16 [16384, 768], P(('dp', 'tensor')), may hold values from -6 to 6
- w_qkv: bfloat16 [3, 768, 768], P(None, 'dp', 'tensor'), may hold values from -0.3125 to 0.3125
- w_out: bfloat16 [768, 768], P('tensor', 'dp'), may hold values from -0.21875 to 0.21875
- conv_weight: float32 [12, 65], P('tensor'), may hold values from -0.48 to 0.48
- w_up: bfloat16 [768, 3072], P(None, ('dp', 'tensor')), may hold values from -0.21875 to 0.21875
- w_down: bfloat16 [3072, 768], P(('dp', 'tensor')), may hold values from -0.109375 to 0.109375
- norm_gain: bfloat16 [2, 768], P(None, ('dp', 'tensor')), may hold values from 0.5 to 1.5
- norm_bias: bfloat16 [2, 768], P(None, ('dp', 'tensor')), may hold values from -3 to 3
- cotangent: bfloat16 [16384, 768], P(('dp', 'tensor')), may hold values from -6 to 6
- seg_ids: int32 [8, 2048], P('dp'), may hold values from 0 to 3, as said below
- landmark_slot: int32 [8, 2048], P('dp'), may hold values from 0 to 256, as said below
- token_live: int32 [8, 2048], P('dp'), may hold values from 0 to 1, as said below
- slot_live: int32 [8, 256], P('dp'), may hold values from 0 to 1, as said below
Outputs:
- layer_out: bfloat16 [16384, 768], P(('dp', 'tensor'))
- input_grad: float32 [16384, 768], P(('dp', 'tensor'))
- grad_qkv: float32 [3, 768, 768], P(None, 'dp', 'tensor')
- grad_out: float32 [768, 768], P('tensor', 'dp')
- grad_conv: float32 [12, 65], P('tensor')
- grad_up: float32 [768, 3072], P(None, ('dp', 'tensor'))
- grad_down: float32 [3072, 768], P(('dp', 'tensor'))
- grad_gain: float32 [2, 768], P(None, ('dp', 'tensor'))
- grad_bias: float32 [2, 768], P(None, ('dp', 'tensor'))
- proxies: float32 [8, 4, 12], P('dp', None, 'tensor')
Inputs may be any that keep to these rules, and one draw needn't show every extreme that they name: `seg_ids`: document numbers never fall along a row; each document of a row has at least 64 tokens; the tail padding carries the number of the row's last document. `landmark_slot`: each document s of a row uses m_s landmark slots, 32 <= m_s <= 64; a token at offset p of document s, which has n tokens, names slot s * 64 + floor(p * m_s / n); tail padding names 256, which is no slot. `token_live`: the zeros form a tail of at most 256 tokens. `slot_live`: slot s is 1 exactly when the row holds document s // 64 and s % 64 < m of that document.
All inputs are finite; a program needn't handle non-finite values.
Results may differ from a plain program's by a relative error of at most 0.014.
The roundings to bfloat16 on the way count: a program that leaves them out, or rounds other values in their place, can miss the bound.
Values may be sent and summed in bfloat16 or wider, within the bound.
A program may use at most 192 MiB of HBM per device.

v0:
```python
import math

import jax
import jax.numpy as jnp
from jax import lax
from jax.sharding import PartitionSpec as P

HEAD_DIM = 64
LANDMARKS = 64
NEWTON = 6


highest = lax.Precision.HIGHEST
norm_epsilon = 1e-05


def split_up(shard, dim, length):
    before, after = (shard.shape[:dim], shard.shape[dim + 1 :])
    return jnp.moveaxis(shard.reshape(*before, length, -1, *after), dim, 0)


def sum_at_owner(shard, axis, dim):
    pieces = split_up(shard, dim, lax.axis_size(axis))
    arrived = lax.all_to_all(pieces, axis, split_axis=0, concat_axis=0, tiled=True)
    return arrived.astype(jnp.float32).sum(axis=0)


def layer_norm(values, gain_row, bias_row):
    average = jnp.mean(values, axis=-1, keepdims=True)
    centered = values - average
    variance = jnp.mean(centered * centered, axis=-1, keepdims=True)
    return centered * lax.rsqrt(variance + norm_epsilon) * gain_row + bias_row


def newton_inverse(query_land, key_land, live_slots):
    scaling = 1.0 / math.sqrt(HEAD_DIM)
    logits = jnp.einsum("...ie,...je->...ij", query_land, key_land, precision=highest) * scaling
    allowed = live_slots[..., None, :] > 0
    weights = (
        jax.nn.softmax(jnp.where(allowed, logits, -1000000000.0), axis=-1)
        * live_slots[..., :, None]
    )
    colsums = jnp.sum(weights, axis=-2)
    initial = 1.0 / jnp.maximum(jnp.max(colsums, axis=-1), 1.0)
    inverse = initial[..., None, None] * jnp.swapaxes(weights, -1, -2)
    identity = jnp.eye(LANDMARKS, dtype=jnp.float32)
    for repeat in range(NEWTON):
        product = jnp.einsum("...ij,...jk->...ik", weights, inverse, precision=highest)
        nested = 7.0 * identity - product
        nested = 15.0 * identity - jnp.einsum(
            "...ij,...jk->...ik", product, nested, precision=highest
        )
        nested = 13.0 * identity - jnp.einsum(
            "...ij,...jk->...ik", product, nested, precision=highest
        )
        inverse = 0.25 * jnp.einsum("...ij,...jk->...ik", inverse, nested, precision=highest)
    return (weights, inverse)


def masked_softmax(logits, allowed):
    filled = jnp.where(allowed, logits, -1000000000.0)
    largest = jnp.max(filled, axis=-1, keepdims=True)
    raised = jnp.exp(filled - largest)
    return raised / jnp.sum(raised, axis=-1, keepdims=True)


def conv_masks(seg_row, live_row, half_width):
    seg_pad = jnp.pad(seg_row, (half_width, half_width), constant_values=-1)
    live_pad = jnp.pad(live_row, (half_width, half_width))
    length = seg_row.shape[0]
    masks = []
    for tap_index in range(2 * half_width + 1):
        masks.append(
            (
                (seg_pad[tap_index : tap_index + length] == seg_row)
                & (live_pad[tap_index : tap_index + length] > 0)
            ).astype(jnp.float32)
        )
    return masks


def per_device(
    tokens,
    w_qkv,
    w_out,
    conv_weight,
    w_up,
    w_down,
    norm_gain,
    norm_bias,
    cotangent,
    seg_ids,
    landmark_slot,
    token_live,
    slot_live,
):
    scaling = 1.0 / math.sqrt(HEAD_DIM)
    gathered = lax.all_gather(tokens, "tensor", axis=0, tiled=True)
    qkv_full, out_full = (
        lax.all_gather(w_qkv, "dp", axis=1, tiled=True),
        lax.all_gather(w_out, "dp", axis=1, tiled=True),
    )
    up_full, down_full, gains_full, biases_full = (
        lax.all_gather(w_up, ("dp", "tensor"), axis=1, tiled=True),
        lax.all_gather(w_down, ("dp", "tensor"), axis=0, tiled=True),
        lax.all_gather(norm_gain, ("dp", "tensor"), axis=1, tiled=True),
        lax.all_gather(norm_bias, ("dp", "tensor"), axis=1, tiled=True),
    )
    seq_len = gathered.shape[0]
    local_heads = qkv_full.shape[2] // HEAD_DIM
    slot_count = slot_live.shape[1]
    doc_slots = slot_count // LANDMARKS
    projected = jnp.einsum(
        "td,cde->cte", gathered, qkv_full, preferred_element_type=jnp.float32
    ).astype(jnp.bfloat16)
    queries = projected[0].reshape(seq_len, local_heads, HEAD_DIM)
    keys_all = projected[1].reshape(seq_len, local_heads, HEAD_DIM)
    values_all = projected[2].reshape(seq_len, local_heads, HEAD_DIM)
    seg_row = seg_ids[0]
    slot_row = landmark_slot[0]
    live_row = token_live[0]
    slot_mask = slot_live[0]
    slot_ids = jnp.arange(slot_count, dtype=jnp.int32)
    onehot = (slot_row[None, :] == slot_ids[:, None]).astype(jnp.bfloat16)
    onehot_wide = onehot.astype(jnp.float32)
    counts = jnp.maximum(jnp.sum(onehot_wide, axis=1), 1.0)
    query_land = (
        jnp.einsum("st,the->hse", onehot, queries, preferred_element_type=jnp.float32)
        / counts[None, :, None]
    )
    key_land = (
        jnp.einsum("st,the->hse", onehot, keys_all, preferred_element_type=jnp.float32)
        / counts[None, :, None]
    )
    slot_float = slot_mask.astype(jnp.float32)
    token_float = live_row.astype(jnp.float32)
    same_doc = (seg_row[:, None] == (slot_ids // LANDMARKS)[None, :]) & (slot_mask[None, :] > 0)
    allowed_three = same_doc.T & (live_row[None, :] > 0) | (slot_mask[:, None] == 0)
    queries_wide = queries.astype(jnp.float32)
    keys_wide = keys_all.astype(jnp.float32)
    kern_one = masked_softmax(
        jnp.einsum("the,hse->hts", queries_wide, key_land, precision=highest) * scaling,
        same_doc[None],
    )
    kern_one_low = kern_one.astype(jnp.bfloat16)
    kern_three = (
        masked_softmax(
            jnp.einsum("hse,the->hst", query_land, keys_wide, precision=highest) * scaling,
            allowed_three[None],
        )
        * slot_float[None, :, None]
    )
    kern_three_low = kern_three.astype(jnp.bfloat16)
    block_shape = (local_heads, doc_slots, LANDMARKS, HEAD_DIM)
    slot_blocks = slot_float.reshape(doc_slots, LANDMARKS)
    (weights, inverse), newton_pull = jax.vjp(
        lambda query_blocks, key_blocks: newton_inverse(query_blocks, key_blocks, slot_blocks),
        query_land.reshape(block_shape),
        key_land.reshape(block_shape),
    )
    carried = jnp.einsum(
        "hst,the->hse", kern_three_low, values_all, preferred_element_type=jnp.float32
    ).reshape(block_shape)
    mixed_low = (
        jnp.einsum("hdij,hdje->hdie", inverse, carried, precision=highest)
        .reshape(local_heads, slot_count, HEAD_DIM)
        .astype(jnp.bfloat16)
    )
    attended = jnp.einsum(
        "hts,hse->the", kern_one_low, mixed_low, preferred_element_type=jnp.float32
    )
    taps_total = conv_weight.shape[1]
    half_width = taps_total // 2
    tap_masks = conv_masks(seg_row, live_row, half_width)
    values_wide = values_all.astype(jnp.float32)
    values_pad = jnp.pad(values_wide, ((half_width, half_width), (0, 0), (0, 0)))
    conv_out = jnp.zeros_like(values_wide)
    for tap_index in range(taps_total):
        conv_out = (
            conv_out
            + conv_weight[:, tap_index][None, :, None]
            * values_pad[tap_index : tap_index + seq_len]
            * tap_masks[tap_index][:, None, None]
        )
    heads_low = (
        ((attended + conv_out) * token_float[:, None, None])
        .reshape(seq_len, local_heads * HEAD_DIM)
        .astype(jnp.bfloat16)
    )
    partial_out = jnp.dot(heads_low, out_full, preferred_element_type=jnp.float32)
    attention = lax.psum_scatter(
        partial_out.astype(jnp.bfloat16), "tensor", scatter_dimension=0, tiled=True
    ).astype(jnp.float32)
    doc_live = slot_blocks[:, 0]
    norm_weights = jnp.sqrt(jnp.where(doc_live > 0, jnp.sum(weights * weights, axis=(-2, -1)), 1.0))
    norm_inverse = jnp.sqrt(jnp.where(doc_live > 0, jnp.sum(inverse * inverse, axis=(-2, -1)), 1.0))
    proxies = (norm_weights * norm_inverse * doc_live / LANDMARKS).T[None]
    residual_in = tokens.astype(jnp.float32) + attention
    hidden, norm_one_pull = jax.vjp(
        layer_norm,
        residual_in,
        gains_full[0].astype(jnp.float32),
        biases_full[0].astype(jnp.float32),
    )
    hidden_low = hidden.astype(jnp.bfloat16)
    up_proj = jnp.dot(hidden_low, up_full, preferred_element_type=jnp.float32)
    activated, gelu_pull = jax.vjp(lambda inputs: jax.nn.gelu(inputs, approximate=False), up_proj)
    activated_low = activated.astype(jnp.bfloat16)
    down_proj = jnp.dot(activated_low, down_full, preferred_element_type=jnp.float32)
    result, norm_two_pull = jax.vjp(
        layer_norm,
        hidden + down_proj,
        gains_full[1].astype(jnp.float32),
        biases_full[1].astype(jnp.float32),
    )
    layer_out = result.astype(jnp.bfloat16)
    grad_sum, gain_two, bias_two = norm_two_pull(cotangent.astype(jnp.float32))
    grad_sum_low = grad_sum.astype(jnp.bfloat16)
    up_back, down_back = (
        lax.all_gather(w_up, ("dp", "tensor"), axis=1, tiled=True),
        lax.all_gather(w_down, ("dp", "tensor"), axis=0, tiled=True),
    )
    grad_down = jnp.einsum(
        "tf,td->fd", activated_low, grad_sum_low, preferred_element_type=jnp.float32
    )
    grad_act = jnp.einsum("td,fd->tf", grad_sum_low, down_back, preferred_element_type=jnp.float32)
    grad_up_low = gelu_pull(grad_act)[0].astype(jnp.bfloat16)
    grad_up = jnp.einsum("td,tf->df", hidden_low, grad_up_low, preferred_element_type=jnp.float32)
    grad_hidden = grad_sum + jnp.einsum(
        "tf,df->td", grad_up_low, up_back, preferred_element_type=jnp.float32
    )
    grad_pre, gain_one, bias_one = norm_one_pull(grad_hidden)
    grad_attn_low = grad_pre.astype(jnp.bfloat16)
    grad_up_shard, grad_down_shard, gain_shard, bias_shard = (
        lax.psum_scatter(grad_up, ("dp", "tensor"), scatter_dimension=1, tiled=True),
        lax.psum_scatter(grad_down, ("dp", "tensor"), scatter_dimension=0, tiled=True),
        lax.psum_scatter(
            jnp.stack([gain_one, gain_two]), ("dp", "tensor"), scatter_dimension=1, tiled=True
        ),
        lax.psum_scatter(
            jnp.stack([bias_one, bias_two]), ("dp", "tensor"), scatter_dimension=1, tiled=True
        ),
    )
    grad_rows = lax.all_gather(grad_attn_low, "tensor", axis=0, tiled=True)
    grad_out_local = jnp.einsum(
        "tk,td->kd", heads_low, grad_rows, preferred_element_type=jnp.float32
    )
    grad_heads = jnp.einsum(
        "td,kd->tk", grad_rows, out_full, preferred_element_type=jnp.float32
    ).astype(jnp.bfloat16)
    grad_heads = (
        grad_heads.reshape(seq_len, local_heads, HEAD_DIM)
        * live_row.astype(jnp.bfloat16)[:, None, None]
    )
    grad_kern_one = jnp.einsum(
        "the,hse->hts", grad_heads, mixed_low, preferred_element_type=jnp.float32
    )
    grad_mixed = jnp.einsum(
        "hts,the->hse", kern_one_low, grad_heads, preferred_element_type=jnp.float32
    ).reshape(block_shape)
    grad_logit_one = (
        kern_one * (grad_kern_one - jnp.sum(grad_kern_one * kern_one, axis=-1, keepdims=True))
    ).astype(jnp.bfloat16)
    grad_inverse = jnp.einsum("hdie,hdje->hdij", grad_mixed, carried, precision=highest)
    grad_carried_low = (
        jnp.einsum("hdij,hdie->hdje", inverse, grad_mixed, precision=highest)
        .reshape(local_heads, slot_count, HEAD_DIM)
        .astype(jnp.bfloat16)
    )
    grad_kern_three = jnp.einsum(
        "hse,the->hst", grad_carried_low, values_all, preferred_element_type=jnp.float32
    )
    grad_values = jnp.einsum(
        "hst,hse->the", kern_three_low, grad_carried_low, preferred_element_type=jnp.float32
    )
    grad_logit_three = (
        kern_three
        * (grad_kern_three - jnp.sum(grad_kern_three * kern_three, axis=-1, keepdims=True))
    ).astype(jnp.bfloat16)
    grad_query_blocks, grad_key_blocks = newton_pull((jnp.zeros_like(weights), grad_inverse))
    grad_query_land = (
        grad_query_blocks.reshape(local_heads, slot_count, HEAD_DIM)
        + jnp.einsum("hst,the->hse", grad_logit_three, keys_all, preferred_element_type=jnp.float32)
        * scaling
    )
    grad_key_land = (
        grad_key_blocks.reshape(local_heads, slot_count, HEAD_DIM)
        + jnp.einsum("hts,the->hse", grad_logit_one, queries, preferred_element_type=jnp.float32)
        * scaling
    )
    grad_queries = (
        jnp.einsum("hts,hse->the", grad_logit_one.astype(jnp.float32), key_land, precision=highest)
        * scaling
    )
    grad_queries = grad_queries + jnp.einsum(
        "st,hse->the", onehot_wide, grad_query_land / counts[None, :, None], precision=highest
    )
    grad_keys = (
        jnp.einsum(
            "hst,hse->the", grad_logit_three.astype(jnp.float32), query_land, precision=highest
        )
        * scaling
    )
    grad_keys = grad_keys + jnp.einsum(
        "st,hse->the", onehot_wide, grad_key_land / counts[None, :, None], precision=highest
    )
    grad_conv_out = grad_heads.astype(jnp.float32)
    grad_pad = jnp.zeros((seq_len + 2 * half_width, local_heads, HEAD_DIM), jnp.float32)
    conv_columns = []
    for tap_index in range(taps_total):
        weighted = grad_conv_out * tap_masks[tap_index][:, None, None]
        conv_columns.append(
            jnp.sum(weighted * values_pad[tap_index : tap_index + seq_len], axis=(0, 2))
        )
        grad_pad = grad_pad.at[tap_index : tap_index + seq_len].add(
            conv_weight[:, tap_index][None, :, None] * weighted
        )
    grad_values = grad_values + grad_pad[half_width : half_width + seq_len]
    conv_local = jnp.stack(conv_columns, axis=1)
    grad_stack = (
        jnp.stack([grad_queries, grad_keys, grad_values])
        .reshape(3, seq_len, local_heads * HEAD_DIM)
        .astype(jnp.bfloat16)
    )
    grad_qkv_local = jnp.einsum(
        "td,cte->cde", gathered, grad_stack, preferred_element_type=jnp.float32
    )
    grad_rows_in = jnp.einsum(
        "cte,cde->td", grad_stack, qkv_full, preferred_element_type=jnp.float32
    )
    input_grad = grad_pre + lax.psum_scatter(
        grad_rows_in.astype(jnp.bfloat16), "tensor", scatter_dimension=0, tiled=True
    ).astype(jnp.float32)
    grad_qkv, grad_out = (
        sum_at_owner(grad_qkv_local.astype(jnp.bfloat16), "dp", 1),
        sum_at_owner(grad_out_local.astype(jnp.bfloat16), "dp", 1),
    )
    grad_conv = lax.psum(conv_local, "dp")
    return (
        layer_out,
        input_grad,
        grad_qkv,
        grad_out,
        grad_conv,
        grad_up_shard,
        grad_down_shard,
        gain_shard,
        bias_shard,
        proxies,
    )


def solution(mesh):
    return jax.shard_map(
        per_device,
        mesh=mesh,
        in_specs=(
            P(("dp", "tensor"), None),
            P(None, "dp", "tensor"),
            P("tensor", "dp"),
            P("tensor", None),
            P(None, ("dp", "tensor")),
            P(("dp", "tensor"), None),
            P(None, ("dp", "tensor")),
            P(None, ("dp", "tensor")),
            P(("dp", "tensor"), None),
            P("dp", None),
            P("dp", None),
            P("dp", None),
            P("dp", None),
        ),
        out_specs=(
            P(("dp", "tensor"), None),
            P(("dp", "tensor"), None),
            P(None, "dp", "tensor"),
            P("tensor", "dp"),
            P("tensor", None),
            P(None, ("dp", "tensor")),
            P(("dp", "tensor"), None),
            P(None, ("dp", "tensor")),
            P(None, ("dp", "tensor")),
            P("dp", None, "tensor"),
        ),
        check_vma=False,
    )
```

profile of v0, /device:TPU:0, one launch (start us, length us, event | category | flops | bytes accessed | tf_op | source)
XLA Modules:
  0.0 1464.3 jit_solution(12020860259545721184)
XLA Ops:
  23.5 34.8 %all_gather.28 = bf16[192,768]{0,1:T(8,128)(2,1)} all-gather(bf16[192,96]{0,1:T(8,128)(2,1)S(1)} %copy.262), channel_id=1, replica_groups=mesh['dp'=8,'tensor'=4] {'dp'}, dimensions={1}, use_global_device_ids=true | all-gather | bytes 331776 | tf_op jit(solution)/shard_map/all_gather | solution.py:101
  65.0 37.8 %all_gather.26 = bf16[3,768,192]{2,0,1:T(4,128)(2,1)S(1)} all-gather(bf16[3,96,192]{2,0,1:T(4,128)(2,1)S(1)} %copy.249), channel_id=1, replica_groups=mesh['dp'=8,'tensor'=4] {'dp'}, dimensions={1}, use_global_device_ids=true | all-gather | bytes 995328 | tf_op jit(solution)/shard_map/all_gather | solution.py:100
  154.4 29.8 %fusion.34 = bf16[2048,3,64]{0,2,1:T(8,128)(2,1)S(1)} fusion(bf16[3,256,64]{2,1,0:T(8,128)(2,1)S(1)} %bitcast.488, f32[2048]{0:T(1024)} %get-tuple-element.1064, f32[2048]{0:T(1024)S(1)} %get-tuple-element.1066, f32[3]{0:T(128)} %get-tuple-element.969, f32[2048]{0:T(1024)S(1)} %copy-done.98, f32[3]{0:T(128)} %get-tuple-element.970, ...), kind=kOutput, calls=%fused_computation.123 | convolution fusion | flops 282329088 | bytes 10101516 | tf_op jit(solution)/shard_map/hts,hse->the/dot_general | solution.py:169
  188.3 39.2 %all-gather = bf16[32,24,2]{1,2,0:T(2,128)(2,1)S(1)} all-gather(bf16[1,24,2]{1,2,0:T(2,128)(2,1)S(1)} %bitcast.568), channel_id=1, replica_groups=mesh['dp'=8,'tensor'=4] {'dp','tensor'}, dimensions={0}, use_global_device_ids=true | all-gather | bytes 3168 | tf_op jit(solution)/shard_map/all_gather | solution.py:106
  229.5 37.0 %all-gather.1 = bf16[32,24,2]{1,2,0:T(2,128)(2,1)S(1)} all-gather(bf16[1,24,2]{1,2,0:T(2,128)(2,1)} %bitcast.569), channel_id=1, replica_groups=mesh['dp'=8,'tensor'=4] {'dp','tensor'}, dimensions={0}, use_global_device_ids=true | all-gather | bytes 3168 | tf_op jit(solution)/shard_map/all_gather | solution.py:107
  273.2 22.2 %multiply_convert_fusion.2 = (bf16[512,3072]{1,0:T(8,128)(2,1)}, f32[512,3072]{1,0:T(8,128)}, f32[512,3072]{1,0:T(8,128)}) fusion(bf16[768,3072]{0,1:T(8,128)(2,1)} %all-gather.9.cloned.1.call-done, f32[768]{0:T(1024)} %get-tuple-element.905, f32[768]{0:T(1024)} %get-tuple-element.1091, f32[512]{0:T(512)} %fusion.649, f32[512]{0:T(512)} %copy-done.214, ...), kind=kOutput, calls=%fused_computation.76 | convolution fusion | flops 2521300992 | bytes 22030336 | tf_op jit(solution)/shard_map/dot_general | solution.py:206
  295.3 29.4 %all-gather.11.cloned.1.call-done = bf16[3072,768]{1,0:T(8,128)(2,1)} async-done(((bf16[96,768]{1,0:T(8,128)(2,1)}), bf16[3072,768]{1,0:T(8,128)(2,1)}) %all-gather.11.cloned.1.call-update) | async-done | bytes 4718608 | tf_op jit(solution)/shard_map/all_gather | solution.py:105
  335.1 8.6 add_convert_fusion
  354.5 24.9 %all-gather.13.cloned.1.call-done = bf16[2048,768]{1,0:T(8,128)(2,1)} async-done(((bf16[512,768]{1,0:T(8,128)(2,1)}), bf16[2048,768]{1,0:T(8,128)(2,1)}) %all-gather.13.cloned.1.call-update) | async-done | bytes 3145744 | tf_op jit(solution)/shard_map/all_gather | solution.py:244
  441.1 8.0 scatter-add.219
  450.8 7.8 scatter-add.220
  460.2 7.8 scatter-add.221
  484.4 7.8 scatter-add.225
  493.8 7.8 scatter-add.226
  503.3 7.8 scatter-add.229
  546.3 7.8 scatter-add.235
  580.4 7.8 scatter-add.240
  633.0 7.8 scatter-add.249
  647.1 7.8 scatter-add.250
  656.6 8.0 scatter-add.251
  689.9 7.8 scatter-add.256
  732.4 7.8 scatter-add.264
  760.7 8.0 scatter-add.269
  784.6 7.8 scatter-add.271
  870.7 8.2 scatter-add.285
  976.1 8.0 scatter-add.301
  1135.9 8.8 fusion.657
  1146.1 8.4 fusion.661
  1181.7 47.5 %all-reduce.6 = (f32[2,768]{1,0:T(2,128)S(1)}, f32[2,768]{1,0:T(2,128)S(1)}) all-reduce(f32[2,768]{1,0:T(2,128)S(1)} %pad_maximum_fusion.3, f32[2,768]{1,0:T(2,128)S(1)} %pad_maximum_fusion.4), channel_id=6, replica_groups=mesh['dp'=8,'tensor'=4] {'dp','tensor'}, use_global_device_ids=true, to_apply=%region_97.98.clone | all-reduce | flops 3072 | bytes 24576
  1244.5 22.4 %psum.7 = f32[3,65]{1,0:T(4,128)} all-reduce(f32[3,65]{1,0:T(4,128)S(1)} %stack.289), channel_id=1, replica_groups=mesh['dp'=8,'tensor'=4] {'dp'}, use_global_device_ids=true, to_apply=%region_92.93 | all-reduce | flops 195 | bytes 1560 | tf_op jit(solution)/shard_map/psum | solution.py:338
  1271.3 43.7 %reduce-scatter.13.cloned.1.call-done = f32[96,768]{1,0:T(8,128)} async-done(((f32[3072,768]{1,0:T(8,128)}), f32[96,768]{1,0:T(8,128)}) %reduce-scatter.13.cloned.1.call-update) | async-done | bytes 294928 | tf_op jit(solution)/shard_map/reduce_scatter | solution.py:236
  1315.0 141.7 %reduce-scatter.11.cloned.1.call-done = f32[768,96]{0,1:T(8,128)} async-done(((f32[768,3072]{0,1:T(8,128)}), f32[768,96]{0,1:T(8,128)}) %reduce-scatter.11.cloned.1.call-update) | async-done | bytes 294928 | tf_op jit(solution)/shard_map/reduce_scatter | solution.py:235
  (1108 shorter events, 773.4 us)
Async XLA Ops:
  8.0 97.5 %all-gather.7.cloned.1.call-start = ((), (), s32[]{:S(2)}) async-start(), calls=%async_computation.6 | async-start | bytes 3932160 | tf_op jit(solution)/shard_map/all_gather | solution.py:98
  8.8 261.1 %reduce-scatter.7.cloned.1.call-start = ((), (), s32[]{:S(2)}) async-start(), calls=%async_computation.7 | async-start | bytes 3932160 | tf_op jit(solution)/shard_map/reduce_scatter | solution.py:191
  11.6 128.5 %copy-start.207 = (f32[4,64]{1,0:T(4,128)}, f32[4,64]{1,0:T(4,128)S(1)}, u32[]{:S(2)}) copy-start(f32[4,64]{1,0:T(4,128)S(1)} %convert_element_type.366) | copy-start | bytes 3076
  23.5 117.4 %copy-start.27 = (f32[64,64]{1,0:T(8,128)}, f32[64,64]{1,0:T(8,128)S(1)}, u32[]{:S(2)}) copy-start(f32[64,64]{1,0:T(8,128)S(1)} %get-tuple-element.1089) | copy-start | bytes 49156
  58.6 63.9 %copy-start.334 = (pred[4,64]{1,0:T(4,128)(4,1)}, pred[4,64]{1,0:T(4,128)(4,1)S(1)}, u32[]{:S(2)}) copy-start(pred[4,64]{1,0:T(4,128)(4,1)S(1)} %broadcast_compare_fusion.1) | copy-start | bytes 772
  143.5 286.2 %copy-start = (f32[2048,3,64]{0,2,1:T(8,128)}, f32[2048,3,64]{0,2,1:T(8,128)S(1)}, u32[]{:S(2)}) copy-start(f32[2048,3,64]{0,2,1:T(8,128)S(1)} %convert_element_type.376) | copy-start | bytes 4718596
  187.0 82.9 %copy-start.13 = (bf16[512,768]{1,0:T(8,128)(2,1)S(1)}, bf16[512,768]{1,0:T(8,128)(2,1)}, u32[]{:S(2)}) copy-start(bf16[512,768]{1,0:T(8,128)(2,1)} %param.143) | copy-start | bytes 2359300
  187.0 86.1 %all-gather.9.cloned.1.call-start = ((), (), s32[]{:S(2)}) async-start(), calls=%async_computation.8 | async-start | bytes 4866048 | tf_op jit(solution)/shard_map/all_gather | solution.py:104
  187.6 137.1 %all-gather.11.cloned.1.call-start = ((), (), s32[]{:S(2)}) async-start(), calls=%async_computation.9 | async-start | bytes 4866048 | tf_op jit(solution)/shard_map/all_gather | solution.py:105
  188.2 191.1 %all-gather.13.cloned.1.call-start = ((), (), s32[]{:S(2)}) async-start(), calls=%async_computation.10 | async-start | bytes 3932160 | tf_op jit(solution)/shard_map/all_gather | solution.py:244
  352.4 916.4 %reduce-scatter.9.cloned.1.call-start = ((), (), s32[]{:S(2)}) async-start(), calls=%async_computation.11 | async-start | bytes 3932160 | tf_op jit(solution)/shard_map/reduce_scatter | solution.py:331
  1134.5 180.4 %reduce-scatter.13.cloned.1.call-start = ((), (), s32[]{:S(2)}) async-start(), calls=%async_computation.13 | async-start | bytes 9732096 | tf_op jit(solution)/shard_map/reduce_scatter | solution.py:236
  1144.7 311.9 %reduce-scatter.11.cloned.1.call-start = ((), (), s32[]{:S(2)}) async-start(), calls=%async_computation.12 | async-start | bytes 9732096 | tf_op jit(solution)/shard_map/reduce_scatter | solution.py:235
  1159.7 17.6 %all-to-all-start.1 = ((bf16[8,192,96]{2,1,0:T(8,128)(2,1)}), bf16[8,192,96]{2,1,0:T(8,128)(2,1)S(1)}, u32[]{:S(2)}, u32[]{:S(2)}) async-start(bf16[8,192,96]{2,1,0:T(8,128)(2,1)} %bitcast.358), calls=%async_computation.3 | async-start | bytes 786432 | tf_op jit(solution)/shard_map/all_to_all | solution.py:24
  1172.3 60.7 %copy-start.313 = (f32[3]{0:T(128)S(1)}, f32[3]{0:T(128)}, u32[]{:S(2)}) copy-start(f32[3]{0:T(128)} %get-tuple-element.844) | copy-start | bytes 40
  1172.3 60.8 %copy-start.312 = (f32[3]{0:T(128)S(1)}, f32[3]{0:T(128)}, u32[]{:S(2)}) copy-start(f32[3]{0:T(128)} %get-tuple-element.845) | copy-start | bytes 40
  1172.3 60.9 %copy-start.311 = (f32[3]{0:T(128)S(1)}, f32[3]{0:T(128)}, u32[]{:S(2)}) copy-start(f32[3]{0:T(128)} %get-tuple-element.846) | copy-start | bytes 40
  1172.3 61.0 %copy-start.320 = (f32[3]{0:T(128)S(1)}, f32[3]{0:T(128)}, u32[]{:S(2)}) copy-start(f32[3]{0:T(128)} %get-tuple-element.848) | copy-start | bytes 40
  1172.3 61.1 %copy-start.319 = (f32[3]{0:T(128)S(1)}, f32[3]{0:T(128)}, u32[]{:S(2)}) copy-start(f32[3]{0:T(128)} %get-tuple-element.847) | copy-start | bytes 40
  1172.3 61.2 %copy-start.318 = (f32[3]{0:T(128)S(1)}, f32[3]{0:T(128)}, u32[]{:S(2)}) copy-start(f32[3]{0:T(128)} %get-tuple-element.849) | copy-start | bytes 40
  1172.3 61.3 %copy-start.317 = (f32[3]{0:T(128)S(1)}, f32[3]{0:T(128)}, u32[]{:S(2)}) copy-start(f32[3]{0:T(128)} %get-tuple-element.850) | copy-start | bytes 40
  1172.3 61.3 %copy-start.316 = (f32[3]{0:T(128)S(1)}, f32[3]{0:T(128)}, u32[]{:S(2)}) copy-start(f32[3]{0:T(128)} %get-tuple-element.851) | copy-start | bytes 40
  1172.3 63.3 %copy-start.329 = (f32[3]{0:T(128)S(1)}, f32[3]{0:T(128)}, u32[]{:S(2)}) copy-start(f32[3]{0:T(128)} %get-tuple-element.873) | copy-start | bytes 40
  1172.3 63.4 %copy-start.328 = (f32[3]{0:T(128)S(1)}, f32[3]{0:T(128)}, u32[]{:S(2)}) copy-start(f32[3]{0:T(128)} %get-tuple-element.872) | copy-start | bytes 40
  1172.4 63.5 %copy-start.327 = (f32[3]{0:T(128)S(1)}, f32[3]{0:T(128)}, u32[]{:S(2)}) copy-start(f32[3]{0:T(128)} %get-tuple-element.874) | copy-start | bytes 40
  1172.4 64.4 %copy-start.333 = (f32[3]{0:T(128)S(1)}, f32[3]{0:T(128)}, u32[]{:S(2)}) copy-start(f32[3]{0:T(128)} %get-tuple-element.877) | copy-start | bytes 40
  1172.4 64.5 %copy-start.332 = (f32[3]{0:T(128)S(1)}, f32[3]{0:T(128)}, u32[]{:S(2)}) copy-start(f32[3]{0:T(128)} %get-tuple-element.879) | copy-start | bytes 40
  1172.4 64.6 %copy-start.331 = (f32[3]{0:T(128)S(1)}, f32[3]{0:T(128)}, u32[]{:S(2)}) copy-start(f32[3]{0:T(128)} %get-tuple-element.880) | copy-start | bytes 40
  1172.4 64.7 %copy-start.330 = (f32[3]{0:T(128)S(1)}, f32[3]{0:T(128)}, u32[]{:S(2)}) copy-start(f32[3]{0:T(128)} %get-tuple-element.881) | copy-start | bytes 40
  1177.3 90.3 %all-to-all-start = ((bf16[8,3,96,192]{2,3,1,0:T(8,128)(2,1)}), bf16[8,3,96,192]{2,3,1,0:T(8,128)(2,1)S(1)}, u32[]{:S(2)}, u32[]{:S(2)}) async-start(bf16[8,3,96,192]{2,3,1,0:T(8,128)(2,1)} %bitcast.357), calls=%async_computation.2 | async-start | bytes 2359296 | tf_op jit(solution)/shard_map/all_to_all | solution.py:24
  1181.7 87.0 %copy-start.2 = (f32[512,768]{1,0:T(8,128)S(1)}, f32[512,768]{1,0:T(8,128)}, u32[]{:S(2)}) copy-start(f32[512,768]{1,0:T(8,128)} %copy-done.1) | copy-start | bytes 4718596
  1181.7 87.0 %copy-start.213 = (f32[512]{0:T(512)S(1)}, f32[512]{0:T(512)}, u32[]{:S(2)}) copy-start(f32[512]{0:T(512)} %copy-done.212) | copy-start | bytes 6148
  (333 other events, 2870.4 us)
Sparse Core Ops, SparseCore 0:
  10.4 31.2 all-gather.6
  187.1 37.1 reduce-scatter.6
  352.5 26.7 all-gather.12
  1134.6 37.9 reduce-scatter.8
  1179.0 135.9 reduce-scatter.12
  1322.3 134.2 reduce-scatter.10
Sparse Core Ops, SparseCore 1:
  190.4 68.8 all-gather.8
  262.5 62.2 all-gather.10
where the time goes:
time: 1480 us; the launch traced here: 1460 us
  local copies, waits for them, and re-layouts  548 us (37%)
  waiting for transfers between devices  246 us (17%)
  blocking collectives  219 us (15%)
  other arithmetic  213 us (14%)
  matrix products  207 us (14%)
  between operations  21 us (1%)
    scatter-add x65, local copies, waits for them, and re-layouts, per_device(): grad_pad.at[tap_index:tap_index + seq_len]  496 us
    reduce_scatter x1, waiting for transfers between devices, per_device(): lax.psum_scatter(grad_up, ('dp', 'tensor'), scatter_dimension=1, tiled=True)  142 us
    reduce_sum x14, other arithmetic, per_device(): jnp.sum(weighted * values_pad[tap_index:tap_index + seq_len], axis=(0, 2))  85 us
    add x52, other arithmetic, per_device(): grad_pad.at[tap_index:tap_index + seq_len]  84.4 us
    unnamed x1, blocking collectives  47.5 us
    reduce_scatter x1, waiting for transfers between devices, per_device(): lax.psum_scatter(grad_down, ('dp', 'tensor'), scatter_dimension=0, tiled=...  43.7 us
    all_gather x1, blocking collectives, per_device(): lax.all_gather(norm_gain, ('dp', 'tensor'), axis=1, tiled=True)  39.2 us
    all_gather x1, blocking collectives, per_device(): lax.all_gather(w_qkv, 'dp', axis=1, tiled=True)  37.8 us
  transfers between devices with their start and end apart: 10, of which 5 were waited for; matrix products, arithmetic and copies ran while one was open for 7% of the time, Pallas kernels for 0%

commit v1 on v0

--- a/solution.py
+++ b/solution.py
@@ -64,19 +64,41 @@
     return raised / jnp.sum(raised, axis=-1, keepdims=True)
 
 
-def conv_masks(seg_row, live_row, half_width):
-    seg_pad = jnp.pad(seg_row, (half_width, half_width), constant_values=-1)
-    live_pad = jnp.pad(live_row, (half_width, half_width))
-    length = seg_row.shape[0]
-    masks = []
-    for tap_index in range(2 * half_width + 1):
-        masks.append(
-            (
-                (seg_pad[tap_index : tap_index + length] == seg_row)
-                & (live_pad[tap_index : tap_index + length] > 0)
-            ).astype(jnp.float32)
-        )
-    return masks
+TILE = 128
+
+
+def band_of(kernel, taps_total):
+    wide = TILE + taps_total - 1
+    row = jnp.pad(kernel, ((0, 0), (0, wide + 1 - taps_total)))
+    flat = jnp.tile(row, (1, TILE))[:, : TILE * wide]
+    return flat.reshape(kernel.shape[0], TILE, wide)
+
+
+def taps_of(band, taps_total):
+    heads, _, wide = band.shape
+    flat = jnp.pad(band.reshape(heads, TILE * wide), ((0, 0), (0, TILE)))
+    return flat.reshape(heads, TILE, wide + 1).sum(axis=1)[:, :taps_total]
+
+
+def windows(rows, half_width):
+    count = rows.shape[0] // TILE
+    pad = [(half_width, half_width)] + [(0, 0)] * (rows.ndim - 1)
+    padded = jnp.pad(rows, pad)
+    return jnp.stack(
+        [padded[i * TILE : i * TILE + TILE + 2 * half_width] for i in range(count)]
+    )
+
+
+def overlap_add(tiles, half_width):
+    count, wide = tiles.shape[:2]
+    rest = tiles.shape[2:]
+    zero = jnp.zeros((1, half_width) + rest, tiles.dtype)
+    body = tiles[:, half_width : half_width + TILE]
+    before = jnp.concatenate([tiles[1:, :half_width], zero])
+    after = jnp.concatenate([zero, tiles[:-1, half_width + TILE :]])
+    gap = jnp.zeros((count, TILE - 2 * half_width) + rest, tiles.dtype)
+    total = body + jnp.concatenate([after, gap, before], axis=1)
+    return total.reshape((count * TILE,) + rest)
 
 
 def per_device(
@@ -96,16 +118,18 @@
 ):
     scaling = 1.0 / math.sqrt(HEAD_DIM)
     gathered = lax.all_gather(tokens, "tensor", axis=0, tiled=True)
-    qkv_full, out_full = (
-        lax.all_gather(w_qkv, "dp", axis=1, tiled=True),
-        lax.all_gather(w_out, "dp", axis=1, tiled=True),
-    )
-    up_full, down_full, gains_full, biases_full = (
+    projections = lax.all_gather(
+        jnp.concatenate([w_qkv, w_out.T[None]]), "dp", axis=1, tiled=True
+    )
+    qkv_full, out_full = projections[:3], projections[3].T
+    up_full, down_full, norms_full = (
         lax.all_gather(w_up, ("dp", "tensor"), axis=1, tiled=True),
         lax.all_gather(w_down, ("dp", "tensor"), axis=0, tiled=True),
-        lax.all_gather(norm_gain, ("dp", "tensor"), axis=1, tiled=True),
-        lax.all_gather(norm_bias, ("dp", "tensor"), axis=1, tiled=True),
-    )
+        lax.all_gather(
+            jnp.concatenate([norm_gain, norm_bias]), ("dp", "tensor"), axis=1, tiled=True
+        ),
+    )
+    gains_full, biases_full = norms_full[:2], norms_full[2:]
     seq_len = gathered.shape[0]
     local_heads = qkv_full.shape[2] // HEAD_DIM
     slot_count = slot_live.shape[1]
@@ -171,17 +195,19 @@
     )
     taps_total = conv_weight.shape[1]
     half_width = taps_total // 2
-    tap_masks = conv_masks(seg_row, live_row, half_width)
-    values_wide = values_all.astype(jnp.float32)
-    values_pad = jnp.pad(values_wide, ((half_width, half_width), (0, 0), (0, 0)))
-    conv_out = jnp.zeros_like(values_wide)
-    for tap_index in range(taps_total):
-        conv_out = (
-            conv_out
-            + conv_weight[:, tap_index][None, :, None]
-            * values_pad[tap_index : tap_index + seq_len]
-            * tap_masks[tap_index][:, None, None]
-        )
+    seg_windows = windows(seg_row + 1, half_width)
+    live_windows = windows(live_row, half_width)
+    tap_mask = (
+        ((seg_row + 1).reshape(-1, TILE)[:, :, None] == seg_windows[:, None, :])
+        & (live_windows[:, None, :] > 0)
+    ).astype(jnp.bfloat16)
+    band = band_of(conv_weight, taps_total)
+    band_low = band.astype(jnp.bfloat16)
+    masked_band = band_low[:, None] * tap_mask[None]
+    value_windows = windows(values_all, half_width)
+    conv_out = jnp.einsum(
+        "hntu,nuhe->nthe", masked_band, value_windows, preferred_element_type=jnp.float32
+    ).reshape(seq_len, local_heads, HEAD_DIM)
     heads_low = (
         ((attended + conv_out) * token_float[:, None, None])
         .reshape(seq_len, local_heads * HEAD_DIM)
@@ -216,10 +242,7 @@
     layer_out = result.astype(jnp.bfloat16)
     grad_sum, gain_two, bias_two = norm_two_pull(cotangent.astype(jnp.float32))
     grad_sum_low = grad_sum.astype(jnp.bfloat16)
-    up_back, down_back = (
-        lax.all_gather(w_up, ("dp", "tensor"), axis=1, tiled=True),
-        lax.all_gather(w_down, ("dp", "tensor"), axis=0, tiled=True),
-    )
+    up_back, down_back = up_full, down_full
     grad_down = jnp.einsum(
         "tf,td->fd", activated_low, grad_sum_low, preferred_element_type=jnp.float32
     )
@@ -231,16 +254,26 @@
     )
     grad_pre, gain_one, bias_one = norm_one_pull(grad_hidden)
     grad_attn_low = grad_pre.astype(jnp.bfloat16)
-    grad_up_shard, grad_down_shard, gain_shard, bias_shard = (
-        lax.psum_scatter(grad_up, ("dp", "tensor"), scatter_dimension=1, tiled=True),
-        lax.psum_scatter(grad_down, ("dp", "tensor"), scatter_dimension=0, tiled=True),
+    grad_up_shard, grad_down_shard = (
         lax.psum_scatter(
-            jnp.stack([gain_one, gain_two]), ("dp", "tensor"), scatter_dimension=1, tiled=True
+            grad_up.astype(jnp.bfloat16), ("dp", "tensor"), scatter_dimension=1, tiled=True
+        ).astype(jnp.float32),
+        lax.psum_scatter(
+            grad_down.astype(jnp.bfloat16), ("dp", "tensor"), scatter_dimension=0, tiled=True
+        ).astype(jnp.float32),
+    )
+    norm_grads = lax.all_to_all(
+        split_up(
+            jnp.stack([gain_one, gain_two, bias_one, bias_two]),
+            1,
+            lax.axis_size("dp") * lax.axis_size("tensor"),
         ),
-        lax.psum_scatter(
-            jnp.stack([bias_one, bias_two]), ("dp", "tensor"), scatter_dimension=1, tiled=True
-        ),
-    )
+        ("dp", "tensor"),
+        split_axis=0,
+        concat_axis=0,
+        tiled=True,
+    ).sum(axis=0)
+    gain_shard, bias_shard = norm_grads[:2], norm_grads[2:]
     grad_rows = lax.all_gather(grad_attn_low, "tensor", axis=0, tiled=True)
     grad_out_local = jnp.einsum(
         "tk,td->kd", heads_low, grad_rows, preferred_element_type=jnp.float32
@@ -304,19 +337,17 @@
     grad_keys = grad_keys + jnp.einsum(
         "st,hse->the", onehot_wide, grad_key_land / counts[None, :, None], precision=highest
     )
-    grad_conv_out = grad_heads.astype(jnp.float32)
-    grad_pad = jnp.zeros((seq_len + 2 * half_width, local_heads, HEAD_DIM), jnp.float32)
-    conv_columns = []
-    for tap_index in range(taps_total):
-        weighted = grad_conv_out * tap_masks[tap_index][:, None, None]
-        conv_columns.append(
-            jnp.sum(weighted * values_pad[tap_index : tap_index + seq_len], axis=(0, 2))
-        )
-        grad_pad = grad_pad.at[tap_index : tap_index + seq_len].add(
-            conv_weight[:, tap_index][None, :, None] * weighted
-        )
-    grad_values = grad_values + grad_pad[half_width : half_width + seq_len]
-    conv_local = jnp.stack(conv_columns, axis=1)
+    head_tiles = grad_heads.reshape(-1, TILE, local_heads, HEAD_DIM)
+    band_grad = jnp.einsum(
+        "nthe,nuhe->nhtu", head_tiles, value_windows, preferred_element_type=jnp.float32
+    )
+    conv_local = taps_of((band_grad * tap_mask[:, None]).sum(axis=0), taps_total)
+    grad_values = grad_values + overlap_add(
+        jnp.einsum(
+            "hntu,nthe->nuhe", masked_band, head_tiles, preferred_element_type=jnp.float32
+        ),
+        half_width,
+    )
     grad_stack = (
         jnp.stack([grad_queries, grad_keys, grad_values])
         .reshape(3, seq_len, local_heads * HEAD_DIM)
@@ -335,7 +366,13 @@
         sum_at_owner(grad_qkv_local.astype(jnp.bfloat16), "dp", 1),
         sum_at_owner(grad_out_local.astype(jnp.bfloat16), "dp", 1),
     )
-    grad_conv = lax.psum(conv_local, "dp")
+    grad_conv = lax.all_to_all(
+        jnp.broadcast_to(conv_local, (lax.axis_size("dp"),) + conv_local.shape),
+        "dp",
+        split_axis=0,
+        concat_axis=0,
+        tiled=True,
+    ).sum(axis=0)
     return (
         layer_out,
         input_grad,

time: 1480 us -> 603 us (0.41)
  local copies, waits for them, and re-layouts: 548 us -> 44.4 us
  blocking collectives: 219 us -> 40.6 us
  other arithmetic: 213 us -> 41.5 us
  matrix products: 207 us -> 175 us
    scatter-add x65 -> x0, local copies, waits for them, and re-layouts: 496 us -> none  [per_device(): grad_pad.at[tap_index:tap_index + seq_len]]
    reduce_scatter x2, waiting for transfers between devices: 185 us -> 34.7 us  [the longest x1 34.7 us: per_device(): lax.psum_scatter(grad_down.astype(jnp.bfloat16), ('dp', 'tensor'), scatte...]
    all_gather x4 -> x1, blocking collectives: 149 us -> 40.6 us  [per_device(): lax.all_gather(jnp.concatenate([norm_gain, norm_bias]), ('dp', 'tensor'),...]
    add x53 -> x2, other arithmetic: 85.8 us -> 0.01 us  [per_device(): seg_row + 1]
    reduce_sum x14 -> x3, other arithmetic: 85 us -> 0.69 us  [the longest x1 0.6 us: per_device(): grad_conv = lax.all_to_all(jnp.broadcast_to(conv_local, (lax.axis_size('d...]
    unnamed x1 -> x0, blocking collectives: 47.5 us -> none
    reduce_scatter x1, waiting for transfers between devices: 0.01 us -> 38 us  [per_device(): lax.psum_scatter(grad_rows_in.astype(jnp.bfloat16), 'tensor', scatter_dim...]
    all_gather x0 -> x1, waiting for transfers between devices: none -> 35.8 us  [per_device(): lax.all_gather(jnp.concatenate([w_qkv, w_out.T[None]]), 'dp', axis=1, til...]
  transfers between devices with their start and end apart: 10 -> 13, of which waited for: 5 -> 11; matrix products, arithmetic and copies ran while one was open for 7% -> 28% of each run, Pallas kernels for 0% -> 0%
where the time goes in v1:
time: 603 us; the launch traced here: 594 us
  waiting for transfers between devices  257 us (43%)
  matrix products  175 us (29%)
  local copies, waits for them, and re-layouts  44.4 us (7%)
  other arithmetic  41.5 us (7%)
  blocking collectives  40.6 us (7%)
  between operations  19.1 us (3%)
  starting transfers between devices  16.1 us (3%)
    all_gather x1, waiting for transfers between devices, per_device(): lax.all_gather(w_down, ('dp', 'tensor'), axis=0, tiled=True)  45.6 us
    all_gather x1, blocking collectives, per_device(): lax.all_gather(jnp.concatenate([norm_gain, norm_bias]), ('dp', 'tensor'),...  40.6 us
    all_to_all x2, waiting for transfers between devices, sum_at_owner(): lax.all_to_all(pieces, axis, split_axis=0, concat_axis=0, tiled=True)  39.5 us
    reduce_scatter x1, waiting for transfers between devices, per_device(): lax.psum_scatter(grad_rows_in.astype(jnp.bfloat16), 'tensor', scatter_dim...  38 us
    all_gather x1, waiting for transfers between devices, per_device(): lax.all_gather(jnp.concatenate([w_qkv, w_out.T[None]]), 'dp', axis=1, til...  35.8 us
    reduce_scatter x1, waiting for transfers between devices, per_device(): lax.psum_scatter(grad_down.astype(jnp.bfloat16), ('dp', 'tensor'), scatte...  34.7 us
    unnamed x376, local copies, waits for them, and re-layouts  26.5 us
    all_gather x1, waiting for transfers between devices, per_device(): lax.all_gather(w_up, ('dp', 'tensor'), axis=1, tiled=True)  26.1 us
  transfers between devices with their start and end apart: 13, of which 11 were waited for; matrix products, arithmetic and copies ran while one was open for 28% of the time, Pallas kernels for 0%

profile of v1, /device:TPU:0, one launch (start us, length us, event | category | flops | bytes accessed | tf_op | source)
XLA Modules:
  0.0 594.0 jit_solution(10117007237365828271)
XLA Ops:
  22.8 35.8 %all-gather.7.cloned.1.call-done = bf16[4,768,192]{2,0,1:T(4,128)(2,1)} async-done(((bf16[4,96,192]{2,0,1:T(4,128)(2,1)}), bf16[4,768,192]{2,0,1:T(4,128)(2,1)}) %all-gather.7.cloned.1.call-update) | async-done | bytes 1179664 | tf_op jit(solution)/shard_map/all_gather | solution.py:121
  58.6 3.5 copy.423
  64.6 23.0 %all-gather.9.cloned.1.call-done = bf16[2048,768]{1,0:T(8,128)(2,1)} async-done(((bf16[512,768]{1,0:T(8,128)(2,1)}), bf16[2048,768]{1,0:T(8,128)(2,1)}) %all-gather.9.cloned.1.call-update) | async-done | bytes 3145744 | tf_op jit(solution)/shard_map/all_gather | solution.py:120
  87.6 4.2 fusion.28
  94.9 4.6 fusion.198
  99.7 4.6 fusion.199
  146.7 40.6 %all-gather = bf16[32,24,4]{1,2,0:T(4,128)(2,1)S(1)} all-gather(bf16[1,24,4]{1,2,0:T(4,128)(2,1)S(1)} %maximum_bitcast_fusion.1), channel_id=1, replica_groups=mesh['dp'=8,'tensor'=4] {'dp','tensor'}, dimensions={0}, use_global_device_ids=true | all-gather | bytes 6336 | tf_op jit(solution)/shard_map/all_gather | solution.py:128
  192.8 26.1 %all-gather.11.cloned.1.call-done = bf16[768,3072]{0,1:T(8,128)(2,1)} async-done(((bf16[768,96]{0,1:T(8,128)(2,1)}), bf16[768,3072]{0,1:T(8,128)(2,1)}) %all-gather.11.cloned.1.call-update) | async-done | bytes 4718608 | tf_op jit(solution)/shard_map/all_gather | solution.py:126
  218.9 19.8 %multiply_convert_fusion.2 = (bf16[512,3072]{1,0:T(8,128)(2,1)}, f32[512,3072]{1,0:T(8,128)}, f32[512,3072]{1,0:T(8,128)}) fusion(bf16[768,3072]{0,1:T(8,128)(2,1)} %all-gather.11.cloned.1.call-done, f32[768]{0:T(1024)} %get-tuple-element.80, f32[768]{0:T(1024)} %get-tuple-element.81, f32[512]{0:T(512)} %fusion.163, f32[512]{0:T(512)} %copy-done.129, ...), kind=kOutput, calls=%fused_computation.11 | convolution fusion | flops 2521300992 | bytes 22030336 | tf_op jit(solution)/shard_map/dot_general | solution.py:232
  238.7 45.6 %all-gather.13.cloned.1.call-done = bf16[3072,768]{1,0:T(8,128)(2,1)} async-done(((bf16[96,768]{1,0:T(8,128)(2,1)}), bf16[3072,768]{1,0:T(8,128)(2,1)}) %all-gather.13.cloned.1.call-update) | async-done | bytes 4718608 | tf_op jit(solution)/shard_map/all_gather | solution.py:127
  284.3 6.5 %fusion.197 = (f32[512]{0:T(512)S(1)}, f32[512,768]{1,0:T(8,128)S(1)}) fusion(bf16[512,3072]{1,0:T(8,128)(2,1)} %get-tuple-element.90, bf16[3072,768]{1,0:T(8,128)(2,1)} %all-gather.13.cloned.1.call-done, f32[768]{0:T(1024)} %get-tuple-element.80, f32[768]{0:T(1024)} %get-tuple-element.81, f32[512]{0:T(512)} %fusion.163, f32[512]{0:T(512)} %copy-done.129, ...), kind=kOutput, calls=%fused_computation.364 | convolution fusion | flops 2419457536 | bytes 11022336 | tf_op jit(solution)/shard_map/dot_general | solution.py:235
  294.1 9.0 %add_convert_fusion = bf16[512,3072]{1,0:T(8,128)(2,1)} fusion(f32[512,3072]{1,0:T(8,128)} %get-tuple-element.91, f32[512,3072]{1,0:T(8,128)} %get-tuple-element.156, bf16[3072,768]{1,0:T(8,128)(2,1)S(1)} %copy-done.162, f32[512,768]{1,0:T(8,128)S(1)} %get-tuple-element.89, f32[512]{0:T(512)S(1)} %negate_multiply_fusion.2), kind=kOutput, calls=%fused_computation.10 | convolution fusion | flops 2438725632 | bytes 22022144 | tf_op jit(solution)/shard_map/td,fd->tf/dot_general | solution.py:249
  303.2 5.5 multiply_reduce_fusion.3
  311.2 7.4 %convolution_convert_fusion.1 = bf16[768,3072]{0,1:T(8,128)(2,1)} fusion(bf16[512,3072]{1,0:T(8,128)(2,1)} %add_convert_fusion, f32[768]{0:T(1024)} %get-tuple-element.80, f32[768]{0:T(1024)} %get-tuple-element.81, f32[512]{0:T(512)} %fusion.163, bf16[512,768]{1,0:T(8,128)(2,1)} %reduce-scatter.5.cloned.1.call-done, bf16[512,768]{1,0:T(8,128)(2,1)} %param.13, ...), kind=kOutput, calls=%fused_computation.31 | convolution fusion | flops 2421424128 | bytes 9447424 | tf_op jit(solution)/shard_map/td,tf->df/dot_general | solution.py:251
  322.5 7.4 %convolution_convert_fusion = bf16[3072,768]{1,0:T(8,128)(2,1)} fusion(bf16[512,3072]{1,0:T(8,128)(2,1)} %get-tuple-element.90, f32[512,768]{1,0:T(8,128)} %copy-done.76, f32[512]{0:T(512)} %copy-done.157), kind=kOutput, calls=%fused_computation.30 | convolution fusion | flops 2419064832 | bytes 9439232 | tf_op jit(solution)/shard_map/tf,td->fd/dot_general | solution.py:246
  330.1 8.0 %all-gather.15.cloned.1.call-done = bf16[2048,768]{1,0:T(8,128)(2,1)} async-done(((bf16[512,768]{1,0:T(8,128)(2,1)}), bf16[2048,768]{1,0:T(8,128)(2,1)}) %all-gather.15.cloned.1.call-update) | async-done | bytes 3145744 | tf_op jit(solution)/shard_map/all_gather | solution.py:277
  338.1 3.2 convolution_convert_fusion.3
  341.4 4.2 fusion.59
  387.3 3.4 multiply_convert_fusion.1
  397.0 3.1 fusion.107
  401.2 4.0 multiply_reduce_fusion
  418.2 4.1 bitcast_convert_fusion
  424.0 4.9 all-to-all-start.3
  428.9 3.1 multiply_reduce_fusion.2
  436.9 3.4 all-to-all-start.2
  440.3 2.8 convolution_convert_fusion.4
  446.8 3.6 all-to-all-start.1
  450.5 5.4 fusion.73
  462.0 3.6 all-to-all-start
  469.6 37.0 %all-to-all-done = bf16[8,3,96,192]{2,3,1,0:T(8,128)(2,1)S(1)} async-done(((bf16[8,3,96,192]{2,3,1,0:T(8,128)(2,1)}), bf16[8,3,96,192]{2,3,1,0:T(8,128)(2,1)S(1)}, u32[]{:S(2)}, u32[]{:S(2)}) %all-to-all-start) | async-done | bytes 884768 | tf_op jit(solution)/shard_map/all_to_all | solution.py:24
  509.4 34.7 %reduce-scatter.11.cloned.1.call-done = bf16[96,768]{1,0:T(8,128)(2,1)} async-done(((bf16[3072,768]{1,0:T(8,128)(2,1)}), bf16[96,768]{1,0:T(8,128)(2,1)}) %reduce-scatter.11.cloned.1.call-update) | async-done | bytes 147472 | tf_op jit(solution)/shard_map/reduce_scatter | solution.py:261
  545.7 38.0 %reduce-scatter.7.cloned.1.call-done = bf16[512,768]{1,0:T(8,128)(2,1)} async-done(((bf16[2048,768]{1,0:T(8,128)(2,1)}), bf16[512,768]{1,0:T(8,128)(2,1)}) %reduce-scatter.7.cloned.1.call-update) | async-done | bytes 786448 | tf_op jit(solution)/shard_map/reduce_scatter | solution.py:362
  (597 shorter events, 164.7 us)
Async XLA Ops:
  8.1 50.6 %all-gather.7.cloned.1.call-start = ((), (), s32[]{:S(2)}) async-start(), calls=%async_computation.8 | async-start | bytes 1769472 | tf_op jit(solution)/shard_map/all_gather | solution.py:121
  11.1 76.5 %all-gather.9.cloned.1.call-start = ((), (), s32[]{:S(2)}) async-start(), calls=%async_computation.9 | async-start | bytes 3932160 | tf_op jit(solution)/shard_map/all_gather | solution.py:120
  11.8 176.2 %reduce-scatter.5.cloned.1.call-start = ((), (), s32[]{:S(2)}) async-start(), calls=%async_computation.10 | async-start | bytes 3932160 | tf_op jit(solution)/shard_map/reduce_scatter | solution.py:217
  13.9 104.9 %copy-start.122 = (f32[4,64]{1,0:T(4,128)}, f32[4,64]{1,0:T(4,128)S(1)}, u32[]{:S(2)}) copy-start(f32[4,64]{1,0:T(4,128)S(1)} %convert_element_type.202) | copy-start | bytes 3076
  16.6 103.5 %copy-start.64 = (f32[64,64]{1,0:T(8,128)}, f32[64,64]{1,0:T(8,128)S(1)}, u32[]{:S(2)}) copy-start(f32[64,64]{1,0:T(8,128)S(1)} %fusion.157) | copy-start | bytes 49156
  16.7 102.9 %copy-start.23 = (f32[64,64]{1,0:T(8,128)}, f32[64,64]{1,0:T(8,128)S(1)}, u32[]{:S(2)}) copy-start(f32[64,64]{1,0:T(8,128)S(1)} %get-tuple-element.170) | copy-start | bytes 49156
  16.7 102.9 %copy-start.66 = (f32[64,64]{1,0:T(8,128)}, f32[64,64]{1,0:T(8,128)S(1)}, u32[]{:S(2)}) copy-start(f32[64,64]{1,0:T(8,128)S(1)} %get-tuple-element.171) | copy-start | bytes 49156
  17.0 77.3 %copy-start.158 = (f32[256]{0:T(256)}, f32[256]{0:T(256)S(1)}, u32[]{:S(2)}) copy-start(f32[256]{0:T(256)S(1)} %broadcast_maximum_fusion) | copy-start | bytes 3076
  17.0 87.5 %copy-start.153 = (pred[4,64]{1,0:T(4,128)(4,1)}, pred[4,64]{1,0:T(4,128)(4,1)S(1)}, u32[]{:S(2)}) copy-start(pred[4,64]{1,0:T(4,128)(4,1)S(1)} %broadcast_compare_fusion.2) | copy-start | bytes 772
  91.9 40.8 %copy-start.5 = (bf16[1,2048,192]{1,2,0:T(8,128)(2,1)}, bf16[1,2048,192]{1,2,0:T(8,128)(2,1)S(1)}, u32[]{:S(2)}) copy-start(bf16[1,2048,192]{1,2,0:T(8,128)(2,1)S(1)} %get-tuple-element.108) | copy-start | bytes 2359300
  94.9 9.5 %copy-start.60 = (f32[3,64,256]{2,1,0:T(8,128)}, f32[3,64,256]{2,1,0:T(8,128)S(1)}, u32[]{:S(2)}) copy-start(f32[3,64,256]{2,1,0:T(8,128)S(1)} %fusion.101) | copy-start | bytes 589828
  145.4 42.6 %copy-start.2 = (bf16[512,768]{1,0:T(8,128)(2,1)S(1)}, bf16[512,768]{1,0:T(8,128)(2,1)}, u32[]{:S(2)}) copy-start(bf16[512,768]{1,0:T(8,128)(2,1)} %param.13) | copy-start | bytes 2359300
  145.4 73.5 %all-gather.11.cloned.1.call-start = ((), (), s32[]{:S(2)}) async-start(), calls=%async_computation.11 | async-start | bytes 4866048 | tf_op jit(solution)/shard_map/all_gather | solution.py:126
  146.0 138.3 %all-gather.13.cloned.1.call-start = ((), (), s32[]{:S(2)}) async-start(), calls=%async_computation.12 | async-start | bytes 4866048 | tf_op jit(solution)/shard_map/all_gather | solution.py:127
  146.6 191.6 %all-gather.15.cloned.1.call-start = ((), (), s32[]{:S(2)}) async-start(), calls=%async_computation.13 | async-start | bytes 3932160 | tf_op jit(solution)/shard_map/all_gather | solution.py:277
  188.0 30.9 %copy-start.7 = (bf16[512,768]{1,0:T(8,128)(2,1)S(1)}, bf16[512,768]{1,0:T(8,128)(2,1)}, u32[]{:S(2)}) copy-start(bf16[512,768]{1,0:T(8,128)(2,1)} %reduce-scatter.5.cloned.1.call-done) | copy-start | bytes 2359300
  292.4 10.7 %slice-start.8 = ((s8[4718592]{0:T(1024)(128)(4,1)}), s8[4194304]{0:T(1024)(128)(4,1)S(1)}, s32[]{:S(2)}) async-start(s8[4718592]{0:T(1024)(128)(4,1)} %bitcast.456), calls=%async_computation.25 | async-start | bytes 8388608
  294.0 9.1 %copy-start.3 = (bf16[512,768]{1,0:T(8,128)(2,1)S(1)}, bf16[512,768]{1,0:T(8,128)(2,1)}, u32[]{:S(2)}) copy-start(bf16[512,768]{1,0:T(8,128)(2,1)} %param.13) | copy-start | bytes 2359300
  294.0 9.1 %copy-start.8 = (bf16[512,768]{1,0:T(8,128)(2,1)S(1)}, bf16[512,768]{1,0:T(8,128)(2,1)}, u32[]{:S(2)}) copy-start(bf16[512,768]{1,0:T(8,128)(2,1)} %reduce-scatter.5.cloned.1.call-done) | copy-start | bytes 2359300
  294.0 9.1 %copy-start.130 = (f32[512]{0:T(512)S(1)}, f32[512]{0:T(512)}, u32[]{:S(2)}) copy-start(f32[512]{0:T(512)} %copy-done.129) | copy-start | bytes 6148
  311.2 196.5 %reduce-scatter.9.cloned.1.call-start = ((), (), s32[]{:S(2)}) async-start(), calls=%async_computation.15 | async-start | bytes 4866048 | tf_op jit(solution)/shard_map/reduce_scatter | solution.py:258
  318.7 225.4 %reduce-scatter.11.cloned.1.call-start = ((), (), s32[]{:S(2)}) async-start(), calls=%async_computation.16 | async-start | bytes 4866048 | tf_op jit(solution)/shard_map/reduce_scatter | solution.py:261
  329.9 11.4 %copy-start.150 = (bf16[2048]{0:T(1024)(128)(2,1)S(1)}, bf16[2048]{0:T(1024)(128)(2,1)}, u32[]{:S(2)}) copy-start(bf16[2048]{0:T(1024)(128)(2,1)} %get-tuple-element.114) | copy-start | bytes 12292
  329.9 253.8 %reduce-scatter.7.cloned.1.call-start = ((), (), s32[]{:S(2)}) async-start(), calls=%async_computation.14 | async-start | bytes 3932160 | tf_op jit(solution)/shard_map/reduce_scatter | solution.py:362
  341.3 36.8 %copy-start.87 = (bf16[2048,192]{0,1:T(8,128)(2,1)}, bf16[2048,192]{0,1:T(8,128)(2,1)S(1)}, u32[]{:S(2)}) copy-start(bf16[2048,192]{0,1:T(8,128)(2,1)S(1)} %convolution_convert_fusion.3) | copy-start | bytes 2359300
  367.7 10.4 %slice-start.6 = ((s8[6291456]{0:T(1024)(128)(4,1)}), s8[4194304]{0:T(1024)(128)(4,1)S(1)}, s32[]{:S(2)}) async-start(s8[6291456]{0:T(1024)(128)(4,1)} %bitcast.367), calls=%async_computation.23 | async-start | bytes 8388608
  424.0 12.3 %all-to-all-start.3 = ((f32[32,4,24]{2,1,0:T(4,128)}), f32[32,4,24]{2,1,0:T(4,128)S(1)}, u32[]{:S(2)}, u32[]{:S(2)}) async-start(f32[32,4,24]{2,1,0:T(4,128)} %copy.375), calls=%async_computation.7 | async-start | bytes 131072 | tf_op jit(solution)/shard_map/all_to_all | solution.py:265
  436.9 9.9 %all-to-all-start.2 = ((f32[8,1,195]{2,1,0:T(1,128)}), f32[8,1,195]{2,1,0:T(1,128)S(1)}, u32[]{:S(2)}, u32[]{:S(2)}) async-start(f32[8,1,195]{2,1,0:T(1,128)} %reshape.625), calls=%async_computation.4 | async-start | bytes 16384 | tf_op jit(solution)/shard_map/all_to_all | solution.py:369
  440.3 10.1 %copy-start.90 = (bf16[2048,3,64]{0,2,1:T(8,128)(2,1)S(1)}, bf16[2048,3,64]{0,2,1:T(8,128)(2,1)}, u32[]{:S(2)}) copy-start(bf16[2048,3,64]{0,2,1:T(8,128)(2,1)} %copy-done.89) | copy-start | bytes 2359300
  446.8 15.2 %all-to-all-start.1 = ((bf16[8,192,96]{2,1,0:T(8,128)(2,1)}), bf16[8,192,96]{2,1,0:T(8,128)(2,1)S(1)}, u32[]{:S(2)}, u32[]{:S(2)}) async-start(bf16[8,192,96]{2,1,0:T(8,128)(2,1)} %bitcast.350), calls=%async_computation.3 | async-start | bytes 786432 | tf_op jit(solution)/shard_map/all_to_all | solution.py:24
  462.0 44.5 %all-to-all-start = ((bf16[8,3,96,192]{2,3,1,0:T(8,128)(2,1)}), bf16[8,3,96,192]{2,3,1,0:T(8,128)(2,1)S(1)}, u32[]{:S(2)}, u32[]{:S(2)}) async-start(bf16[8,3,96,192]{2,3,1,0:T(8,128)(2,1)} %bitcast.349), calls=%async_computation.2 | async-start | bytes 2359296 | tf_op jit(solution)/shard_map/all_to_all | solution.py:24
  465.7 118.1 %copy-start.128 = (f32[512]{0:T(512)S(1)}, f32[512]{0:T(512)}, u32[]{:S(2)}) copy-start(f32[512]{0:T(512)} %copy-done.127) | copy-start | bytes 6148
  (156 other events, 504.7 us)
Sparse Core Ops, SparseCore 0:
  11.6 46.9 all-gather.6
  60.2 27.3 all-gather.8
  145.5 38.3 reduce-scatter.4
  311.3 26.7 all-gather.14
Sparse Core Ops, SparseCore 1:
  148.8 70.1 all-gather.10
  222.1 62.1 all-gather.12
  318.7 104.8 reduce-scatter.8
  429.1 114.9 reduce-scatter.10
  546.8 36.9 reduce-scatter.6
